TPU v7x, 256 devices: a whole 4x4x8 slice. The times are simulated.
256 devices in a mesh: rows: 64 (over y, z, core), tau: 4 (over x).
Axes of the slice: x: 4, y: 4, z: 8, core: 2. Of those that a mesh axis runs over, the one named last changes fastest.
Arguments:
- chi_grad: bfloat16 [4, 8192, 8192], P('tau', 'rows'), may hold values from -6 to 6
- green_unocc: bfloat16 [4, 8192, 8192], P('tau', 'rows'), may hold values from -6 to 6
- orbitals: bfloat16 [8192, 1536], P('rows'), may hold values from -0.0625 to 0.0625
- tau_points: float32 [4], P('tau'), may hold values from 0.1 to 2
- energy: float32 [1536], replicated, may hold values from 0.05 to 2
Outputs:
- orbital_grad: float32 [8192, 1536], P('rows', 'tau')
All inputs are finite; a program needn't handle non-finite values.
Results may differ from a plain program's by a relative error of at most 0.0029.
Values may be sent and summed in bfloat16 or wider, within the bound.
A program may use at most 192 MiB of HBM per device.

v0:
```python
import jax
import jax.numpy as jnp
from jax import lax
from jax.sharding import PartitionSpec as P


def per_device(chi_grad, green_unocc, orbitals, tau_points, energy):
    occ_grad = (chi_grad.astype(jnp.float32) * green_unocc.astype(jnp.float32)).astype(jnp.bfloat16)
    weights = jnp.exp(-tau_points[:, None] * energy[None, :])
    swapped = lax.all_to_all(occ_grad, "rows", split_axis=2, concat_axis=1, tiled=True)
    extra = 0.0
    block_rows = lax.all_gather(orbitals, "rows", axis=0, tiled=True)
    running = jnp.einsum("trc,cn->trn", occ_grad, block_rows, preferred_element_type=jnp.float32)
    running = running + jnp.einsum(
        "tcr,cn->trn", swapped, block_rows, preferred_element_type=jnp.float32
    )
    summed = jnp.sum(running * weights[:, None, :], axis=0) + extra
    return lax.psum_scatter(summed, "tau", scatter_dimension=1, tiled=True)


def solution(mesh):
    return jax.shard_map(
        per_device,
        mesh=mesh,
        in_specs=(P("tau", "rows", None), P("tau", "rows", None), P("rows", None), P("tau"), P()),
        out_specs=P("rows", "tau"),
        check_vma=False,
    )
```

profile of v0, /device:TPU:1, one launch (start us, length us, event | category | flops | bytes accessed | tf_op | source)
XLA Modules:
  0.0 227.2 jit_solution(3609215445079688112)
XLA Ops:
  6.5 0.0 all-gather.2.cloned.1.call-start
  6.5 0.7 all-gather.2.cloned.1.call-update
  7.3 2.7 %multiply_convert_fusion = bf16[1,128,8192]{2,1,0:T(8,128)(2,1)S(1)} fusion(bf16[1,128,8192]{2,1,0:T(8,128)(2,1)} %param.6, bf16[1,128,8192]{2,1,0:T(8,128)(2,1)} %param.5), kind=kLoop, calls=%fused_computation | loop fusion | flops 4194304 | bytes 6291456 | tf_op jit(solution)/shard_map/convert_element_type | solution.py:8
  10.0 7.0 %copy.12 = bf16[1,128,8192]{1,0,2:T(2,128)(2,1)} copy(bf16[1,128,8192]{2,1,0:T(8,128)(2,1)S(1)} %multiply_convert_fusion) | data formatting | bytes 4194304 | tf_op jit(solution)/shard_map/convert_element_type | solution.py:8
  16.9 0.5 broadcast.5
  17.5 46.5 %reduce = bf16[8192,128]{1,0:T(8,128)(2,1)} reduce(bf16[8192,1,128]{2,1,0:T(2,128)(2,1)} %bitcast.13, bf16[]{:T(256)} %broadcast.5), dimensions={1}, to_apply=%bitcast.8.reduce_sub_computation | reduce | bytes 4194306
  64.0 4.1 %reshape.25 = bf16[64,2,8192]{2,1,0:T(2,128)(2,1)} reshape(bf16[8192,128]{1,0:T(8,128)(2,1)} %reduce) | data formatting | bytes 4194304
  68.1 0.0 copy-start.1
  68.1 13.5 %all-to-all-start = ((bf16[64,2,8192]{2,1,0:T(2,128)(2,1)}), bf16[64,2,8192]{2,1,0:T(2,128)(2,1)}, u32[]{:S(2)}, u32[]{:S(2)}) async-start(bf16[64,2,8192]{2,1,0:T(2,128)(2,1)} %reshape.25), calls=%async_computation | async-start | bytes 4194304 | tf_op jit(solution)/shard_map/all_to_all | solution.py:10
  81.6 0.0 reduce-scatter.2.cloned.1.call-start
  82.3 0.0 copy-done.1
  82.3 72.2 %all-to-all-done = bf16[64,2,8192]{2,1,0:T(2,128)(2,1)} async-done(((bf16[64,2,8192]{2,1,0:T(2,128)(2,1)}), bf16[64,2,8192]{2,1,0:T(2,128)(2,1)}, u32[]{:S(2)}, u32[]{:S(2)}) %all-to-all-start) | async-done | bytes 2097184 | tf_op jit(solution)/shard_map/all_to_all | solution.py:10
  154.6 10.5 %reshape.26 = bf16[8192,1,128]{2,1,0:T(2,128)(2,1)} reshape(bf16[64,2,8192]{2,1,0:T(2,128)(2,1)} %all-to-all-done) | data formatting | bytes 4194304
  165.1 3.9 %copy.14 = bf16[1,128,8192]{1,2,0:T(8,128)(2,1)} copy(bf16[1,128,8192]{1,0,2:T(2,128)(2,1)} %bitcast.14) | data formatting | bytes 4194304
  169.0 4.1 %copy.13 = bf16[1,64,128,128]{3,2,1,0:T(8,128)(2,1)} copy(bf16[1,64,128,128]{2,3,1,0:T(8,128)(2,1)} %bitcast.16) | data formatting | bytes 4194304 | tf_op jit(solution)/shard_map/all_to_all | solution.py:10
  173.0 3.8 %all-gather.2.cloned.1.call-done = bf16[8192,1536]{1,0:T(8,128)(2,1)} async-done(((bf16[128,1536]{1,0:T(8,128)(2,1)}), bf16[8192,1536]{1,0:T(8,128)(2,1)}) %all-gather.2.cloned.1.call-update) | async-done | bytes 25165840 | tf_op jit(solution)/shard_map/all_gather | solution.py:12
  176.8 0.0 copy-start
  176.8 10.1 %fusion.1 = f32[128,1536]{1,0:T(8,128)S(1)} fusion(bf16[8192,1536]{1,0:T(8,128)(2,1)} %all-gather.2.cloned.1.call-done, bf16[1,128,8192]{2,1,0:T(8,128)(2,1)S(1)} %multiply_convert_fusion), kind=kOutput, calls=%fused_computation.3 | convolution fusion | flops 3221225472 | bytes 28049408 | tf_op jit(solution)/shard_map/trc,cn->trn/dot_general | solution.py:13
  187.0 0.0 copy-done
  187.0 11.1 %fusion = f32[128,1536]{1,0:T(8,128)} fusion(f32[128,1536]{1,0:T(8,128)S(1)} %fusion.1, bf16[8192,128]{1,0:T(8,128)(2,1)S(1)} %bitcast.15, bf16[8192,1536]{1,0:T(8,128)(2,1)} %all-gather.2.cloned.1.call-done, f32[1536]{0:T(1024)S(1)} %multiply_exponential_fusion), kind=kOutput, calls=%fused_computation.2 | convolution fusion | flops 3221618688 | bytes 28841984 | tf_op jit(solution)/shard_map/tcr,cn->trn/dot_general | solution.py:14
  198.0 0.0 reduce-scatter.2.cloned.1.call-update
  198.1 22.3 %reduce-scatter.2.cloned.1.call-done = f32[128,384]{1,0:T(8,128)} async-done(((f32[128,1536]{1,0:T(8,128)}), f32[128,384]{1,0:T(8,128)}) %reduce-scatter.2.cloned.1.call-update) | async-done | bytes 196624 | tf_op jit(solution)/shard_map/reduce_scatter | solution.py:18
  (1 shorter events, 0.0 us)
Async XLA Ops:
  6.5 170.3 %all-gather.2.cloned.1.call-start = ((), (), s32[]{:S(2)}) async-start(), calls=%async_computation.2 | async-start | bytes 25559040 | tf_op jit(solution)/shard_map/all_gather | solution.py:12
  68.1 14.2 %copy-start.1 = (f32[1536]{0:T(1024)S(1)}, f32[1536]{0:T(1024)}, u32[]{:S(2)}) copy-start(f32[1536]{0:T(1024)} %param.9) | copy-start | bytes 18436
  68.1 86.4 %all-to-all-start = ((bf16[64,2,8192]{2,1,0:T(2,128)(2,1)}), bf16[64,2,8192]{2,1,0:T(2,128)(2,1)}, u32[]{:S(2)}, u32[]{:S(2)}) async-start(bf16[64,2,8192]{2,1,0:T(2,128)(2,1)} %reshape.25), calls=%async_computation | async-start | bytes 4194304 | tf_op jit(solution)/shard_map/all_to_all | solution.py:10
  81.6 138.8 %reduce-scatter.2.cloned.1.call-start = ((), (), s32[]{:S(2)}) async-start(), calls=%async_computation.3 | async-start | bytes 983040 | tf_op jit(solution)/shard_map/reduce_scatter | solution.py:18
  176.8 10.1 %copy-start = (bf16[1,64,128,128]{3,2,1,0:T(8,128)(2,1)S(1)}, bf16[1,64,128,128]{3,2,1,0:T(8,128)(2,1)}, u32[]{:S(2)}) copy-start(bf16[1,64,128,128]{3,2,1,0:T(8,128)(2,1)} %copy.13) | copy-start | bytes 6291460
Sparse Core Ops, SparseCore 0:
  10.1 166.6 all-gather.1
  198.2 22.1 reduce-scatter.1
where the time goes:
time: 228 us; the launch traced here: 227 us
  waiting for transfers between devices  99.1 us (43%)
  other arithmetic  49.2 us (22%)
  local copies, waits for them, and re-layouts  30.1 us (13%)
  matrix products  21.2 us (9%)
  between operations  14.1 us (6%)
  starting transfers between devices  13.5 us (6%)
    all_to_all x1, waiting for transfers between devices, per_device(): lax.all_to_all(occ_grad, 'rows', split_axis=2, concat_axis=1, tiled=True)  72.2 us
    unnamed x1, other arithmetic  46.5 us
    reduce_scatter x1, waiting for transfers between devices, per_device(): return lax.psum_scatter(summed, 'tau', scatter_dimension=1, tiled=True)  22.3 us
    unnamed x8, local copies, waits for them, and re-layouts  19.1 us
    all_to_all x1, starting transfers between devices, per_device(): lax.all_to_all(occ_grad, 'rows', split_axis=2, concat_axis=1, tiled=True)  13.5 us
    dot_general x1, matrix products, per_device(): jnp.einsum('tcr,cn->trn', swapped, block_rows, preferred_element_type=jnp...  11.1 us
    dot_general x1, matrix products, per_device(): jnp.einsum('trc,cn->trn', occ_grad, block_rows, preferred_element_type=jn...  10.1 us
    convert_element_type x1, local copies, waits for them, and re-layouts, per_device(): (chi_grad.astype(jnp.float32) * green_unocc.astype(jnp.float32)).astype(j...  6.97 us
  transfers between devices with their start and end apart: 3, of which 3 were waited for; matrix products, arithmetic and copies ran while one was open for 35% of the time, Pallas kernels for 0%

commit v1 on v0

v1 whole, which is shorter than its diff:
```python
import functools

import jax
import jax.numpy as jnp
from jax import lax
from jax.experimental import pallas as pl
from jax.experimental.pallas import tpu as pltpu
from jax.sharding import PartitionSpec as P

MESH = pl.DeviceIdType.MESH
X, Y, Z, C = 4, 4, 8, 2
ROWS = 128
SUB = ROWS // X
NPTS = ROWS * Y * Z * C
COLS = NPTS // (X * Y)
SPAN = NPTS // Y
NOCC = 1536
NB = NOCC // X
GROUP = X * ROWS


def kernel(
    chi, green, orb, tau, energy, out,
    chi_v, green_v, sbuf, blocks, blocks_t, orb_r, orb_c, scaled_r, scaled_c, taus,
    p1, p2, p2_sib, p2_rx, p2_tx, r1, r2, f_tx, f_rx,
    load_sem, own_sem, tau_s, tau_r, or_s, or_r, oc_s, oc_r, os_s, os_r, aa_s, aa_r,
    p1_s, p1_r, sib_s, sib_r, p2_s, p2_r, f_s, f_r,
):
    x = lax.axis_index("tau")
    row = lax.axis_index("rows")
    y, q = row // (Z * C), row % (Z * C)
    z, c = q // C, q % C

    def at(dx=0, dy=0, dz=0, flip=False):
        core = 1 - c if flip else c
        return (((y + dy) % Y) * (Z * C) + ((z + dz) % Z) * C + core, (x + dx) % X)

    def remote(src, dst, s, r, dev):
        return pltpu.make_async_remote_copy(
            src_ref=src, dst_ref=dst, send_sem=s, recv_sem=r, device_id=dev, device_id_type=MESH
        )

    loads = []
    for dy in range(Y):
        cols = pl.ds(pl.multiple_of(((y + dy) % Y) * SPAN, SPAN), SPAN)
        pair = [
            pltpu.make_async_copy(chi.at[:, cols], chi_v.at[dy], load_sem.at[0, dy]),
            pltpu.make_async_copy(green.at[:, cols], green_v.at[dy], load_sem.at[1, dy]),
        ]
        for cp in pair:
            cp.start()
        loads.append(pair)
    mine = orb.at[pl.ds(pl.multiple_of(x * SUB, SUB), SUB)]
    own = [
        pltpu.make_async_copy(orb, orb_r.at[0], own_sem.at[0]),
        pltpu.make_async_copy(mine, orb_c.at[q], own_sem.at[1]),
    ]
    for cp in own:
        cp.start()

    barrier = pltpu.get_barrier_semaphore()
    for dx in range(X):
        for dy in range(Y):
            if dx or dy:
                pl.semaphore_signal(barrier, inc=1, device_id=at(dx, dy), device_id_type=MESH)
    for dz in range(1, Z):
        pl.semaphore_signal(barrier, inc=1, device_id=at(dz=dz), device_id_type=MESH)
    pl.semaphore_signal(barrier, inc=1, device_id=at(flip=True), device_id_type=MESH)
    pl.semaphore_wait(barrier, X * Y - 1 + Z - 1 + 1)

    sent = []

    def go(cp):
        cp.start()
        sent.append(cp)
        return cp

    orb_r_in = [go(remote(orb, orb_r.at[dy], or_s.at[dy], or_r.at[dy], at(dy=dy))) for dy in range(1, Y)]
    oc_in = [go(remote(mine, orb_c.at[q], oc_s.at[dz], oc_r.at[dz], at(dz=dz))) for dz in range(1, Z)]
    os_in = [go(remote(mine, orb_c.at[q], os_s.at[0], os_r.at[0], at(flip=True)))]
    taus[0] = jnp.full((8, 128), tau[0], jnp.float32)
    tau_in = [go(remote(taus.at[0], taus.at[dx], tau_s.at[dx], tau_r.at[dx], at(dx=dx))) for dx in range(1, X)]

    src = lax.broadcasted_iota(jnp.int32, (GROUP, GROUP), 0)
    dst = lax.broadcasted_iota(jnp.int32, (GROUP, GROUP), 1)
    origin = ((dst // SUB) % X) * ROWS + (dst // ROWS) * SUB + dst % SUB
    sort = jnp.where(src == origin, 1.0, 0.0).astype(jnp.bfloat16)

    aa_in = {}
    for dy in range(Y):
        for cp in loads[dy]:
            cp.wait()
        for g in range(SPAN // GROUP):
            cols = slice(g * GROUP, (g + 1) * GROUP)
            occ = (
                chi_v[dy, :, cols].astype(jnp.float32) * green_v[dy, :, cols].astype(jnp.float32)
            ).astype(jnp.bfloat16)
            packed = jnp.dot(occ, sort, preferred_element_type=jnp.float32).astype(jnp.bfloat16)
            for k in range(X):
                sbuf[dy, k, :, g * ROWS:(g + 1) * ROWS] = packed[:, k * ROWS:(k + 1) * ROWS]
        for dx in range(X):
            part = sbuf.at[dy, (x + dx) % X]
            if dx or dy:
                aa_in[dx, dy] = go(
                    remote(part, blocks.at[dx, dy], aa_s.at[dx, dy], aa_r.at[dx, dy], at(dx, dy))
                )
            else:
                keep = pltpu.make_async_copy(part, blocks.at[0, 0], own_sem.at[2])
                keep.start()

    for cp in own:
        cp.wait()
    for dz in range(1, Z):
        oc_in[dz - 1].wait_recv()
        slot = ((z - dz) % Z) * C + c
        os_in.append(go(remote(orb_c.at[slot], orb_c.at[slot], os_s.at[dz], os_r.at[dz], at(flip=True))))
    for cp in tau_in:
        cp.wait_recv()
    weights = [jnp.exp(-taus[dx][:1, :1] * energy[...]) for dx in range(X)]
    for cp in os_in:
        cp.wait_recv()
    for dx in range(X):
        for k in range(Z * C):
            scaled_c[dx, k * SUB:(k + 1) * SUB] = (orb_c[k].astype(jnp.float32) * weights[dx]).astype(jnp.bfloat16)
    for dy in range(Y):
        if dy:
            orb_r_in[dy - 1].wait_recv()
        for dx in range(X):
            scaled_r[dx * Y + dy] = (orb_r[dy].astype(jnp.float32) * weights[dx]).astype(jnp.bfloat16)

    for dy in range(Y):
        for dx in range(X):
            if dx or dy:
                aa_in[dx, dy].wait_recv()
            else:
                keep.wait()
            k = dx * Y + dy
            blocks_t[:, k * ROWS:(k + 1) * ROWS] = blocks[dx, dy].T

    for n in range(X):
        cols = slice(n * NB, (n + 1) * NB)
        rhs = scaled_r[:, :, cols].reshape(X * Y * ROWS, NB)
        acc = jnp.dot(blocks_t[...], rhs, preferred_element_type=jnp.float32)
        p2[:, :, :, cols] = acc.reshape(Z, C, SUB, NB)
    p2_sib[...] = p2[:, 1 - c].astype(jnp.bfloat16)
    sib = go(remote(p2_sib, p2_rx, sib_s, sib_r, at(flip=True)))

    p1_in = []

    def rows_part(dx):
        cols = pl.ds(pl.multiple_of(((x + dx) % X) * NB, NB), NB)
        acc = jnp.zeros((Y * ROWS, NB), jnp.float32)
        for k in range(X):
            acc += jnp.dot(
                blocks[k].reshape(Y * ROWS, COLS), scaled_c[k, :, cols], preferred_element_type=jnp.float32
            )
        p1[dx] = acc.astype(jnp.bfloat16).reshape(Y, ROWS, NB)
        for dy in range(Y):
            if dx or dy:
                p1_in.append(
                    go(remote(p1.at[dx, dy], r1.at[dx, dy], p1_s.at[dx, dy], p1_r.at[dx, dy], at(dx, -dy)))
                )

    rows_part(1)
    rows_part(2)
    sib.wait_recv()
    p2_tx[...] = (p2[:, c] + p2_rx[...].astype(jnp.float32)).astype(jnp.bfloat16)
    p2_in = [
        go(remote(p2_tx.at[(z + dz) % Z], r2.at[dz], p2_s.at[dz], p2_r.at[dz], at(dz=dz))) for dz in range(1, Z)
    ]
    rows_part(3)
    rows_part(0)

    total = p2_tx[z].astype(jnp.float32)
    for dz in range(1, Z):
        p2_in[dz - 1].wait_recv()
        total += r2[dz].astype(jnp.float32)
    for n in range(X):
        f_tx[n] = total[:, n * NB:(n + 1) * NB]
    f_in = [
        go(remote(f_tx.at[(x + dx) % X], f_rx.at[dx], f_s.at[dx], f_r.at[dx], at(dx=dx))) for dx in range(1, X)
    ]
    total = p1[0, 0].astype(jnp.float32)
    for cp in p1_in:
        cp.wait_recv()
    for dx in range(X):
        for dy in range(Y):
            if dx or dy:
                total += r1[dx, dy].astype(jnp.float32)
    out[...] = total
    out[pl.ds(pl.multiple_of(x * SUB, SUB), SUB)] += f_tx[x]
    for dx in range(1, X):
        f_in[dx - 1].wait_recv()
        out[pl.ds(pl.multiple_of(((x - dx) % X) * SUB, SUB), SUB)] += f_rx[dx]
    for cp in sent:
        cp.wait_send()


def per_device(chi_grad, green_unocc, orbitals, tau_points, energy):
    bf16, f32 = jnp.bfloat16, jnp.float32
    dma, vmem = pltpu.SemaphoreType.DMA, pltpu.VMEM
    hbm = pl.BlockSpec(memory_space=pl.ANY)
    return pl.pallas_call(
        kernel,
        out_shape=jax.ShapeDtypeStruct((ROWS, NB), f32),
        in_specs=[
            hbm, hbm, hbm,
            pl.BlockSpec(memory_space=pltpu.SMEM),
            pl.BlockSpec(memory_space=pltpu.VMEM),
        ],
        out_specs=pl.BlockSpec(memory_space=pltpu.VMEM),
        scratch_shapes=[
            vmem((Y, ROWS, SPAN), bf16), vmem((Y, ROWS, SPAN), bf16),
            vmem((Y, X, ROWS, COLS), bf16), vmem((X, Y, ROWS, COLS), bf16), vmem((COLS, X * Y * ROWS), bf16),
            vmem((Y, ROWS, NOCC), bf16), vmem((Z * C, SUB, NOCC), bf16),
            vmem((X * Y, ROWS, NOCC), bf16), vmem((X, COLS, NOCC), bf16),
            vmem((X, 8, 128), f32),
            vmem((X, Y, ROWS, NB), bf16), vmem((Z, C, SUB, NOCC), f32),
            vmem((Z, SUB, NOCC), bf16), vmem((Z, SUB, NOCC), bf16), vmem((Z, SUB, NOCC), bf16),
            vmem((X, Y, ROWS, NB), bf16), vmem((Z, SUB, NOCC), bf16),
            vmem((X, SUB, NB), f32), vmem((X, SUB, NB), f32),
            dma((2, Y)), dma((3,)), dma((X,)), dma((X,)), dma((Y,)), dma((Y,)), dma((Z,)), dma((Z,)), dma((Z,)), dma((Z,)),
            dma((X, Y)), dma((X, Y)), dma((X, Y)), dma((X, Y)), dma, dma, dma((Z,)), dma((Z,)), dma((X,)), dma((X,)),
        ],
        compiler_params=pltpu.CompilerParams(
            collective_id=1, has_side_effects=True, vmem_limit_bytes=56 * 2**20
        ),
        cost_estimate=pl.CostEstimate(flops=4 * ROWS * NPTS * NOCC, bytes_accessed=5 * 2**20, transcendentals=X * NOCC),
        name="response_backward",
    )(chi_grad[0], green_unocc[0], orbitals, tau_points, energy.reshape(1, NOCC))


def solution(mesh):
    return jax.shard_map(
        per_device,
        mesh=mesh,
        in_specs=(P("tau", "rows", None), P("tau", "rows", None), P("rows", None), P("tau"), P()),
        out_specs=P("rows", "tau"),
        check_vma=False,
    )
```

time: 228 us -> 89.1 us (0.39)
  waiting for transfers between devices: 99.1 us -> 0 us
  Pallas kernels: 0 us -> 85.3 us
  other arithmetic: 49.2 us -> 0 us
  local copies, waits for them, and re-layouts: 30.1 us -> 2.91 us
  matrix products: 21.2 us -> 0 us
  starting transfers between devices: 13.5 us -> 0 us
  between operations: 14.1 us -> 0.66 us
    pallas_call x0 -> x1, Pallas kernels: none -> 85.3 us  [per_device(): pl.pallas_call(kernel, out_shape=jax.ShapeDtypeStruct((ROWS, NB), f32), i...]
    all_to_all x1 -> x0, waiting for transfers between devices: 72.2 us -> none  [per_device(): lax.all_to_all(occ_grad, 'rows', split_axis=2, concat_axis=1, tiled=True)]
    unnamed x1 -> x0, other arithmetic: 46.5 us -> none
    reduce_scatter x1 -> x0, waiting for transfers between devices: 22.3 us -> none  [per_device(): return lax.psum_scatter(summed, 'tau', scatter_dimension=1, tiled=True)]
    dot_general x2 -> x0, matrix products: 21.2 us -> none  [the longest x1 11.1 us: per_device(): jnp.einsum('tcr,cn->trn', swapped, block_rows, preferred_element_type=jnp...]
    unnamed x8 -> x1, local copies, waits for them, and re-layouts: 19.1 us -> 1.62 us
    all_to_all x1 -> x0, starting transfers between devices: 13.5 us -> none  [per_device(): lax.all_to_all(occ_grad, 'rows', split_axis=2, concat_axis=1, tiled=True)]
    convert_element_type x1 -> x0, local copies, waits for them, and re-layouts: 6.97 us -> none  [per_device(): (chi_grad.astype(jnp.float32) * green_unocc.astype(jnp.float32)).astype(j...]
  transfers between devices with their start and end apart: 3 -> 0, of which waited for: 3 -> 0; matrix products, arithmetic and copies ran while one was open for 35% -> 0% of each run, Pallas kernels for 0% -> 0%
where the time goes in v1:
time: 89.1 us; the launch traced here: 88.9 us
  Pallas kernels  85.3 us (96%)
  local copies, waits for them, and re-layouts  2.91 us (3%)
    pallas_call x1, Pallas kernels, per_device(): pl.pallas_call(kernel, out_shape=jax.ShapeDtypeStruct((ROWS, NB), f32), i...  85.3 us

profile of v1, /device:TPU:1, one launch (start us, length us, event | category | flops | bytes accessed | tf_op | source)
XLA Modules:
  0.0 88.9 jit_solution(18182383912542035908)
XLA Ops:
  0.7 1.3 %reshape.3.energy = f32[1,1536]{1,0:T(1,128)} reshape(f32[1536]{0:T(1024)} %param.9) | data formatting | bytes 12288 | tf_op jit(solution)/shard_map/reshape | solution.py:230
  1.9 85.3 %response_backward.1 = f32[128,384]{1,0:T(8,128)} custom-call(bf16[128,8192]{1,0:T(8,128)(2,1)} %bitcast.2, bf16[128,8192]{1,0:T(8,128)(2,1)} %bitcast.3, bf16[128,1536]{1,0:T(8,128)(2,1)} %orb.1, f32[1]{0:T(128)S(6)} %copy.7.tau, f32[1,1536]{1,0:T(1,128)} %reshape.3.energy), custom_call_target="tpu_custom_call" | custom-call | flops 6442450944 | bytes 5242880 | tf_op jit(solution)/shard_map/response_backward/pallas_call | solution.py:203
  87.3 1.6 %copy.8 = f32[128,384]{1,0:T(8,128)} copy(f32[128,384]{1,0:T(8,128)} %response_backward.1) | data formatting | bytes 393216

commit v2 on v0

v2 whole, which is shorter than its diff:
```python
import jax
import jax.numpy as jnp
from jax import lax
from jax.experimental import pallas as pl
from jax.experimental.pallas import tpu as pltpu
from jax.sharding import PartitionSpec as P

MESH = pl.DeviceIdType.MESH
BF16, F32 = jnp.bfloat16, jnp.float32
X, Y, Z, C = 4, 4, 8, 2
ROWS = 128
SUB = ROWS // X
NPTS = ROWS * Y * Z * C
COLS = NPTS // (X * Y)
SPAN = NPTS // Y
NOCC = 1536
NB = NOCC // X
GROUP = X * ROWS


def kernel(
    chi, green, orb, tau, energy, out,
    chi_v, green_v, occ_v, sbuf, blocks, blocks_t, orb_r, orb_c, taus,
    p1, r1x, p1y, r1y, p2, p2_sib, p2_rx, p2_tx, r2, f_tx, f_rx,
    load_sem, own_sem, tau_s, tau_r, or_s, or_r, oc_s, oc_r, os_s, os_r, aa_s, aa_r,
    px_s, px_r, py_s, py_r, sib_s, sib_r, p2_s, p2_r, f_s, f_r,
):
    x = lax.axis_index("tau")
    row = lax.axis_index("rows")
    y, q = row // (Z * C), row % (Z * C)
    z, c = q // C, q % C

    def at(dx=0, dy=0, dz=0, flip=False):
        core = 1 - c if flip else c
        return (((y + dy) % Y) * (Z * C) + ((z + dz) % Z) * C + core, (x + dx) % X)

    def remote(src, dst, s, r, dev):
        return pltpu.make_async_remote_copy(
            src_ref=src, dst_ref=dst, send_sem=s, recv_sem=r, device_id=dev, device_id_type=MESH
        )

    def nblock(k):
        return pl.ds(pl.multiple_of(((x + k) % X) * NB, NB), NB)

    order = (2, 1, 3, 0)
    loads = {}
    for dy in order:
        cols = pl.ds(pl.multiple_of(((y + dy) % Y) * SPAN, SPAN), SPAN)
        loads[dy] = [
            pltpu.make_async_copy(chi.at[:, cols], chi_v.at[dy], load_sem.at[0, dy]),
            pltpu.make_async_copy(green.at[:, cols], green_v.at[dy], load_sem.at[1, dy]),
        ]
        for cp in loads[dy]:
            cp.start()
    mine = orb.at[pl.ds(pl.multiple_of(x * SUB, SUB), SUB)]
    own = [pltpu.make_async_copy(mine, orb_c.at[q], own_sem.at[0])]
    for k in range(X):
        own.append(pltpu.make_async_copy(orb.at[:, nblock(k)], orb_r.at[k, 0], own_sem.at[2 + k]))
    for cp in own:
        cp.start()

    barrier = pltpu.get_barrier_semaphore()
    for dx in range(X):
        for dy in range(Y):
            if dx or dy:
                pl.semaphore_signal(barrier, inc=1, device_id=at(dx, dy), device_id_type=MESH)
    for dz in range(1, Z):
        pl.semaphore_signal(barrier, inc=1, device_id=at(dz=dz), device_id_type=MESH)
    pl.semaphore_signal(barrier, inc=1, device_id=at(flip=True), device_id_type=MESH)

    dst = lax.broadcasted_iota(jnp.int32, (8, GROUP), 1)
    origin = ((dst // SUB) % X) * ROWS + (dst // ROWS) * SUB + dst % SUB
    src = lax.broadcasted_iota(jnp.int32, (GROUP, GROUP), 0)
    sort = jnp.where(src == origin[:1], 1.0, 0.0).astype(BF16)

    def make(dy):
        for cp in loads[dy]:
            cp.wait()
        groups = SPAN // GROUP
        for g in range(groups):
            cols = slice(g * GROUP, (g + 1) * GROUP)
            occ_v[g] = (chi_v[dy, :, cols].astype(F32) * green_v[dy, :, cols].astype(F32)).astype(BF16)
        packed = jnp.dot(occ_v[...].reshape(groups * ROWS, GROUP), sort, preferred_element_type=F32).astype(BF16)
        for g in range(groups):
            for k in range(X):
                sbuf[dy, k, :, g * ROWS:(g + 1) * ROWS] = packed[g * ROWS:(g + 1) * ROWS, k * ROWS:(k + 1) * ROWS]

    sent = []

    def go(cp):
        cp.start()
        sent.append(cp)
        return cp

    aa_in = {}

    def send_blocks(dy):
        for dx in order:
            part = sbuf.at[dy, (x + dx) % X]
            if dx or dy:
                cp = remote(part, blocks.at[dx, dy], aa_s.at[dx, dy], aa_r.at[dx, dy], at(dx, dy))
                cp.start()
                aa_in[dx, dy] = cp
            else:
                keep = pltpu.make_async_copy(part, blocks.at[0, 0], own_sem.at[1])
                keep.start()
                aa_in[0, 0] = keep

    or_in = {}

    def send_orb(k):
        for dy in order[:3]:
            or_in[k, dy] = go(
                remote(orb.at[:, nblock(k)], orb_r.at[k, dy], or_s.at[k, dy], or_r.at[k, dy], at(dy=dy))
            )

    taus[0] = jnp.full((8, 128), tau[0], F32)
    make(2)
    make(1)
    pl.semaphore_wait(barrier, X * Y - 1 + Z - 1 + 1)
    send_blocks(2)
    send_blocks(1)
    oc_in = {
        dz: go(remote(mine, orb_c.at[q], oc_s.at[dz], oc_r.at[dz], at(dz=dz))) for dz in (4, 3, 5, 2, 6, 1, 7)
    }
    os_in = [go(remote(mine, orb_c.at[q], os_s.at[0], os_r.at[0], at(flip=True)))]
    tau_in = [go(remote(taus.at[0], taus.at[dx], tau_s.at[dx], tau_r.at[dx], at(dx=dx))) for dx in range(1, X)]
    make(3)
    send_blocks(3)
    make(0)
    send_blocks(0)
    send_orb(1)

    for cp in own:
        cp.wait()
    for dz in (1, 7, 2, 6, 3, 5, 4):
        oc_in[dz].wait_recv()
        slot = ((z - dz) % Z) * C + c
        os_in.append(go(remote(orb_c.at[slot], orb_c.at[slot], os_s.at[dz], os_r.at[dz], at(flip=True))))
    for cp in tau_in:
        cp.wait_recv()

    def arrive(dx, dy):
        if dx or dy:
            aa_in[dx, dy].wait_recv()
        else:
            aa_in[0, 0].wait()
        blocks_t[dx, :, dy * ROWS:(dy + 1) * ROWS] = blocks[dx, dy].T

    for dx in range(X):
        arrive(dx, 0)
    for cp in os_in:
        cp.wait_recv()
    for dy in (1, 3, 2):
        for dx in range(X):
            arrive(dx, dy)
    for cp in aa_in.values():
        if cp is not aa_in[0, 0]:
            cp.wait_send()
    for k in (2, 3, 0):
        send_orb(k)

    sib_in, p2_in, px_in = {}, {}, {}

    def weight(dx, k):
        return jnp.exp(-taus[dx][:1, :1] * energy[:, nblock(k)])

    def cols_part(k):
        for dy in range(1, Y):
            or_in[k, dy].wait_recv()
        rhs = orb_r[k].reshape(Y * ROWS, NB)
        acc = 0.0
        for dx in range(X):
            acc += jnp.dot(blocks_t[dx], rhs, preferred_element_type=F32) * weight(dx, k)
        p2[k] = acc.reshape(Z, C, SUB, NB)
        p2_sib[k] = p2[k, :, 1 - c].astype(BF16)
        sib_in[k] = go(remote(p2_sib.at[k], p2_rx.at[k], sib_s.at[k], sib_r.at[k], at(flip=True)))

    def cols_send(k):
        sib_in[k].wait_recv()
        p2_tx[k] = (p2[k, :, c] + p2_rx[k].astype(F32)).astype(BF16)
        for dz in (4, 3, 5, 2, 6, 1, 7):
            p2_in[k, dz] = go(
                remote(p2_tx.at[k, (z + dz) % Z], r2.at[k, dz], p2_s.at[k, dz], p2_r.at[k, dz], at(dz=dz))
            )

    def rows_part(k):
        rhs = orb_c[:, :, nblock(k)].reshape(COLS, NB)
        acc = 0.0
        for dx in range(X):
            acc += jnp.dot(blocks[dx].reshape(Y * ROWS, COLS), rhs, preferred_element_type=F32) * weight(dx, k)
        p1[k] = acc.astype(BF16).reshape(Y, ROWS, NB)
        if k:
            px_in[k] = go(remote(p1.at[k], r1x.at[k], px_s.at[k], px_r.at[k], at(dx=k)))

    cols_part(1)
    rows_part(1)
    cols_send(1)
    rows_part(2)
    cols_part(2)
    rows_part(3)
    cols_send(2)
    rows_part(0)
    cols_part(3)
    cols_send(3)
    cols_part(0)
    cols_send(0)

    def cols_sum(k):
        total = p2_tx[k, z].astype(F32)
        for dz in (1, 7, 2, 6, 3, 5, 4):
            p2_in[k, dz].wait_recv()
            total += r2[k, dz].astype(F32)
        f_tx[k] = total
        if k:
            return go(remote(f_tx.at[k], f_rx.at[k], f_s.at[k], f_r.at[k], at(dx=k)))

    f_in = [cols_sum(1)]
    for k in range(1, X):
        px_in[k].wait_recv()
    py_in = []
    for dy in order:
        total = p1[0, dy].astype(F32)
        for k in range(1, X):
            total += r1x[k, dy].astype(F32)
        if dy:
            p1y[dy] = total.astype(BF16)
            py_in.append(go(remote(p1y.at[dy], r1y.at[dy], py_s.at[dy], py_r.at[dy], at(dy=-dy))))
    out[...] = total
    f_in.append(cols_sum(2))
    f_in.append(cols_sum(3))
    for cp in py_in:
        cp.wait_recv()
    out[...] += r1y[1].astype(F32) + r1y[2].astype(F32) + r1y[3].astype(F32)
    for k in range(1, X):
        f_in[k - 1].wait_recv()
        out[pl.ds(pl.multiple_of(((x - k) % X) * SUB, SUB), SUB)] += f_rx[k]
    cols_sum(0)
    out[pl.ds(pl.multiple_of(x * SUB, SUB), SUB)] += f_tx[0]
    for cp in sent:
        cp.wait_send()


def per_device(chi_grad, green_unocc, orbitals, tau_points, energy):
    dma, vmem = pltpu.SemaphoreType.DMA, pltpu.VMEM
    hbm = pl.BlockSpec(memory_space=pl.ANY)
    return pl.pallas_call(
        kernel,
        out_shape=jax.ShapeDtypeStruct((ROWS, NB), F32),
        in_specs=[
            hbm, hbm, hbm,
            pl.BlockSpec(memory_space=pltpu.SMEM),
            pl.BlockSpec(memory_space=pltpu.VMEM),
        ],
        out_specs=pl.BlockSpec(memory_space=pltpu.VMEM),
        scratch_shapes=[
            vmem((Y, ROWS, SPAN), BF16), vmem((Y, ROWS, SPAN), BF16), vmem((SPAN // GROUP, ROWS, GROUP), BF16),
            vmem((Y, X, ROWS, COLS), BF16), vmem((X, Y, ROWS, COLS), BF16), vmem((X, COLS, Y * ROWS), BF16),
            vmem((X, Y, ROWS, NB), BF16), vmem((Z * C, SUB, NOCC), BF16), vmem((X, 8, 128), F32),
            vmem((X, Y, ROWS, NB), BF16), vmem((X, Y, ROWS, NB), BF16),
            vmem((Y, ROWS, NB), BF16), vmem((Y, ROWS, NB), BF16),
            vmem((X, Z, C, SUB, NB), F32), vmem((X, Z, SUB, NB), BF16), vmem((X, Z, SUB, NB), BF16),
            vmem((X, Z, SUB, NB), BF16), vmem((X, Z, SUB, NB), BF16),
            vmem((X, SUB, NB), F32), vmem((X, SUB, NB), F32),
            dma((2, Y)), dma((2 + X,)), dma((X,)), dma((X,)), dma((X, Y)), dma((X, Y)),
            dma((Z,)), dma((Z,)), dma((Z,)), dma((Z,)), dma((X, Y)), dma((X, Y)),
            dma((X,)), dma((X,)), dma((Y,)), dma((Y,)), dma((X,)), dma((X,)),
            dma((X, Z)), dma((X, Z)), dma((X,)), dma((X,)),
        ],
        compiler_params=pltpu.CompilerParams(
            collective_id=1, has_side_effects=True, vmem_limit_bytes=56 * 2**20
        ),
        cost_estimate=pl.CostEstimate(flops=4 * ROWS * NPTS * NOCC, bytes_accessed=5 * 2**20, transcendentals=X * NOCC),
        name="response_backward",
    )(chi_grad[0], green_unocc[0], orbitals, tau_points, energy.reshape(1, NOCC))


def solution(mesh):
    return jax.shard_map(
        per_device,
        mesh=mesh,
        in_specs=(P("tau", "rows", None), P("tau", "rows", None), P("rows", None), P("tau"), P()),
        out_specs=P("rows", "tau"),
        check_vma=False,
    )
```

time: 228 us -> 77.6 us (0.34)
  waiting for transfers between devices: 99.1 us -> 0 us
  Pallas kernels: 0 us -> 73.9 us
  other arithmetic: 49.2 us -> 0 us
  local copies, waits for them, and re-layouts: 30.1 us -> 2.91 us
  matrix products: 21.2 us -> 0 us
  starting transfers between devices: 13.5 us -> 0 us
  between operations: 14.1 us -> 0.66 us
    pallas_call x0 -> x1, Pallas kernels: none -> 73.9 us  [per_device(): pl.pallas_call(kernel, out_shape=jax.ShapeDtypeStruct((ROWS, NB), F32), i...]
    all_to_all x1 -> x0, waiting for transfers between devices: 72.2 us -> none  [per_device(): lax.all_to_all(occ_grad, 'rows', split_axis=2, concat_axis=1, tiled=True)]
    unnamed x1 -> x0, other arithmetic: 46.5 us -> none
    reduce_scatter x1 -> x0, waiting for transfers between devices: 22.3 us -> none  [per_device(): return lax.psum_scatter(summed, 'tau', scatter_dimension=1, tiled=True)]
    dot_general x2 -> x0, matrix products: 21.2 us -> none  [the longest x1 11.1 us: per_device(): jnp.einsum('tcr,cn->trn', swapped, block_rows, preferred_element_type=jnp...]
    unnamed x8 -> x1, local copies, waits for them, and re-layouts: 19.1 us -> 1.62 us
    all_to_all x1 -> x0, starting transfers between devices: 13.5 us -> none  [per_device(): lax.all_to_all(occ_grad, 'rows', split_axis=2, concat_axis=1, tiled=True)]
    convert_element_type x1 -> x0, local copies, waits for them, and re-layouts: 6.97 us -> none  [per_device(): (chi_grad.astype(jnp.float32) * green_unocc.astype(jnp.float32)).astype(j...]
  transfers between devices with their start and end apart: 3 -> 0, of which waited for: 3 -> 0; matrix products, arithmetic and copies ran while one was open for 35% -> 0% of each run, Pallas kernels for 0% -> 0%
where the time goes in v2:
time: 77.6 us; the launch traced here: 77.4 us
  Pallas kernels  73.9 us (95%)
  local copies, waits for them, and re-layouts  2.91 us (4%)
    pallas_call x1, Pallas kernels, per_device(): pl.pallas_call(kernel, out_shape=jax.ShapeDtypeStruct((ROWS, NB), F32), i...  73.9 us
    unnamed x1, local copies, waits for them, and re-layouts  1.62 us

profile of v2, /device:TPU:1, one launch (start us, length us, event | category | flops | bytes accessed | tf_op | source)
XLA Modules:
  0.0 77.4 jit_solution(13368241161834952135)
XLA Ops:
  0.7 1.3 %reshape.3.energy = f32[1,1536]{1,0:T(1,128)} reshape(f32[1536]{0:T(1024)} %param.9) | data formatting | bytes 12288 | tf_op jit(solution)/shard_map/reshape | solution.py:275
  1.9 73.9 %response_backward.1 = f32[128,384]{1,0:T(8,128)} custom-call(bf16[128,8192]{1,0:T(8,128)(2,1)} %bitcast.2, bf16[128,8192]{1,0:T(8,128)(2,1)} %bitcast.3, bf16[128,1536]{1,0:T(8,128)(2,1)} %orb.1, f32[1]{0:T(128)S(6)} %copy.7.tau, f32[1,1536]{1,0:T(1,128)} %reshape.3.energy), custom_call_target="tpu_custom_call" | custom-call | flops 6442450944 | bytes 5242880 | tf_op jit(solution)/shard_map/response_backward/pallas_call | solution.py:247
  75.8 1.6 %copy.8 = f32[128,384]{1,0:T(8,128)} copy(f32[128,384]{1,0:T(8,128)} %response_backward.1) | data formatting | bytes 393216

commit v3 on v2

--- a/solution.py
+++ b/solution.py
@@ -20,7 +20,7 @@
 
 def kernel(
     chi, green, orb, tau, energy, out,
-    chi_v, green_v, occ_v, sbuf, blocks, blocks_t, orb_r, orb_c, taus,
+    chi_v, green_v, occ_v, sbuf, blocks, blocks_t, orb_r, orb_c, taus, levels,
     p1, r1x, p1y, r1y, p2, p2_sib, p2_rx, p2_tx, r2, f_tx, f_rx,
     load_sem, own_sem, tau_s, tau_r, or_s, or_r, oc_s, oc_r, os_s, os_r, aa_s, aa_r,
     px_s, px_r, py_s, py_r, sib_s, sib_r, p2_s, p2_r, f_s, f_r,
@@ -42,9 +42,8 @@
     def nblock(k):
         return pl.ds(pl.multiple_of(((x + k) % X) * NB, NB), NB)
 
-    order = (2, 1, 3, 0)
     loads = {}
-    for dy in order:
+    for dy in (2, 1, 3, 0):
         cols = pl.ds(pl.multiple_of(((y + dy) % Y) * SPAN, SPAN), SPAN)
         loads[dy] = [
             pltpu.make_async_copy(chi.at[:, cols], chi_v.at[dy], load_sem.at[0, dy]),
@@ -56,6 +55,7 @@
     own = [pltpu.make_async_copy(mine, orb_c.at[q], own_sem.at[0])]
     for k in range(X):
         own.append(pltpu.make_async_copy(orb.at[:, nblock(k)], orb_r.at[k, 0], own_sem.at[2 + k]))
+    own.append(pltpu.make_async_copy(energy, levels, own_sem.at[2 + X]))
     for cp in own:
         cp.start()
 
@@ -94,22 +94,19 @@
 
     aa_in = {}
 
-    def send_blocks(dy):
-        for dx in order:
-            part = sbuf.at[dy, (x + dx) % X]
-            if dx or dy:
-                cp = remote(part, blocks.at[dx, dy], aa_s.at[dx, dy], aa_r.at[dx, dy], at(dx, dy))
-                cp.start()
-                aa_in[dx, dy] = cp
-            else:
-                keep = pltpu.make_async_copy(part, blocks.at[0, 0], own_sem.at[1])
-                keep.start()
-                aa_in[0, 0] = keep
+    def send_block(dx, dy):
+        part = sbuf.at[dy, (x + dx) % X]
+        if dx or dy:
+            cp = remote(part, blocks.at[dx, dy], aa_s.at[dx, dy], aa_r.at[dx, dy], at(dx, dy))
+        else:
+            cp = pltpu.make_async_copy(part, blocks.at[0, 0], own_sem.at[1])
+        cp.start()
+        aa_in[dx, dy] = cp
 
     or_in = {}
 
     def send_orb(k):
-        for dy in order[:3]:
+        for dy in (2, 1, 3):
             or_in[k, dy] = go(
                 remote(orb.at[:, nblock(k)], orb_r.at[k, dy], or_s.at[k, dy], or_r.at[k, dy], at(dy=dy))
             )
@@ -117,19 +114,19 @@
     taus[0] = jnp.full((8, 128), tau[0], F32)
     make(2)
     make(1)
+    make(3)
     pl.semaphore_wait(barrier, X * Y - 1 + Z - 1 + 1)
-    send_blocks(2)
-    send_blocks(1)
+    tau_in = [go(remote(taus.at[0], taus.at[dx], tau_s.at[dx], tau_r.at[dx], at(dx=dx))) for dx in range(1, X)]
+    for dx, dy in ((0, 2), (2, 2), (0, 1), (0, 3), (1, 1), (3, 3), (1, 3), (3, 1), (1, 2), (3, 2), (2, 1), (2, 3)):
+        send_block(dx, dy)
+    make(0)
+    for dx in (2, 1, 3, 0):
+        send_block(dx, 0)
+    send_orb(1)
     oc_in = {
         dz: go(remote(mine, orb_c.at[q], oc_s.at[dz], oc_r.at[dz], at(dz=dz))) for dz in (4, 3, 5, 2, 6, 1, 7)
     }
     os_in = [go(remote(mine, orb_c.at[q], os_s.at[0], os_r.at[0], at(flip=True)))]
-    tau_in = [go(remote(taus.at[0], taus.at[dx], tau_s.at[dx], tau_r.at[dx], at(dx=dx))) for dx in range(1, X)]
-    make(3)
-    send_blocks(3)
-    make(0)
-    send_blocks(0)
-    send_orb(1)
 
     for cp in own:
         cp.wait()
@@ -137,6 +134,7 @@
         oc_in[dz].wait_recv()
         slot = ((z - dz) % Z) * C + c
         os_in.append(go(remote(orb_c.at[slot], orb_c.at[slot], os_s.at[dz], os_r.at[dz], at(flip=True))))
+    send_orb(2)
     for cp in tau_in:
         cp.wait_recv()
 
@@ -147,26 +145,13 @@
             aa_in[0, 0].wait()
         blocks_t[dx, :, dy * ROWS:(dy + 1) * ROWS] = blocks[dx, dy].T
 
-    for dx in range(X):
-        arrive(dx, 0)
-    for cp in os_in:
-        cp.wait_recv()
-    for dy in (1, 3, 2):
-        for dx in range(X):
-            arrive(dx, dy)
-    for cp in aa_in.values():
-        if cp is not aa_in[0, 0]:
-            cp.wait_send()
-    for k in (2, 3, 0):
-        send_orb(k)
-
     sib_in, p2_in, px_in = {}, {}, {}
 
     def weight(dx, k):
-        return jnp.exp(-taus[dx][:1, :1] * energy[:, nblock(k)])
+        return jnp.exp(-taus[dx][:1, :1] * levels[nblock(k)].reshape(1, NB))
 
     def cols_part(k):
-        for dy in range(1, Y):
+        for dy in (1, 3, 2):
             or_in[k, dy].wait_recv()
         rhs = orb_r[k].reshape(Y * ROWS, NB)
         acc = 0.0
@@ -191,20 +176,35 @@
             acc += jnp.dot(blocks[dx].reshape(Y * ROWS, COLS), rhs, preferred_element_type=F32) * weight(dx, k)
         p1[k] = acc.astype(BF16).reshape(Y, ROWS, NB)
         if k:
-            px_in[k] = go(remote(p1.at[k], r1x.at[k], px_s.at[k], px_r.at[k], at(dx=k)))
-
-    cols_part(1)
-    rows_part(1)
-    cols_send(1)
-    rows_part(2)
-    cols_part(2)
-    rows_part(3)
-    cols_send(2)
-    rows_part(0)
-    cols_part(3)
-    cols_send(3)
-    cols_part(0)
-    cols_send(0)
+            rows_send(k, 1, Y - 1)
+
+    def rows_send(k, first, count):
+        part = pl.ds(first, count)
+        px_in[k, first] = go(
+            remote(p1.at[k, part], r1x.at[k, part], px_s.at[k, first], px_r.at[k, first], at(dx=k))
+        )
+
+    for dx, dy in aa_in:
+        arrive(dx, dy)
+    for dx, dy in aa_in:
+        if dx or dy:
+            aa_in[dx, dy].wait_send()
+    for cp in os_in:
+        cp.wait_recv()
+    for k in (3, 0):
+        send_orb(k)
+
+    py_in = []
+
+    def rows_sum(dy):
+        total = p1[0, dy].astype(F32)
+        for k in range(1, X):
+            total += r1x[k, dy].astype(F32)
+        if dy:
+            p1y[dy] = total.astype(BF16)
+            py_in.append(go(remote(p1y.at[dy], r1y.at[dy], py_s.at[dy], py_r.at[dy], at(dy=-dy))))
+        else:
+            out[...] = total
 
     def cols_sum(k):
         total = p2_tx[k, z].astype(F32)
@@ -215,20 +215,30 @@
         if k:
             return go(remote(f_tx.at[k], f_rx.at[k], f_s.at[k], f_r.at[k], at(dx=k)))
 
+    cols_part(1)
+    rows_part(2)
+    cols_send(1)
+    rows_part(1)
+    cols_part(2)
+    rows_part(3)
+    cols_send(2)
+    cols_part(3)
+    rows_part(0)
+    cols_send(3)
+    for k in (2, 1, 3):
+        rows_send(k, 0, 1)
+    cols_part(0)
     f_in = [cols_sum(1)]
+    cols_send(0)
     for k in range(1, X):
-        px_in[k].wait_recv()
-    py_in = []
-    for dy in order:
-        total = p1[0, dy].astype(F32)
-        for k in range(1, X):
-            total += r1x[k, dy].astype(F32)
-        if dy:
-            p1y[dy] = total.astype(BF16)
-            py_in.append(go(remote(p1y.at[dy], r1y.at[dy], py_s.at[dy], py_r.at[dy], at(dy=-dy))))
-    out[...] = total
+        px_in[k, 1].wait_recv()
+    for dy in (2, 1, 3):
+        rows_sum(dy)
     f_in.append(cols_sum(2))
     f_in.append(cols_sum(3))
+    for k in range(1, X):
+        px_in[k, 0].wait_recv()
+    rows_sum(0)
     for cp in py_in:
         cp.wait_recv()
     out[...] += r1y[1].astype(F32) + r1y[2].astype(F32) + r1y[3].astype(F32)
@@ -250,21 +260,22 @@
         in_specs=[
             hbm, hbm, hbm,
             pl.BlockSpec(memory_space=pltpu.SMEM),
-            pl.BlockSpec(memory_space=pltpu.VMEM),
+            hbm,
         ],
         out_specs=pl.BlockSpec(memory_space=pltpu.VMEM),
         scratch_shapes=[
             vmem((Y, ROWS, SPAN), BF16), vmem((Y, ROWS, SPAN), BF16), vmem((SPAN // GROUP, ROWS, GROUP), BF16),
             vmem((Y, X, ROWS, COLS), BF16), vmem((X, Y, ROWS, COLS), BF16), vmem((X, COLS, Y * ROWS), BF16),
             vmem((X, Y, ROWS, NB), BF16), vmem((Z * C, SUB, NOCC), BF16), vmem((X, 8, 128), F32),
+            vmem((NOCC,), F32),
             vmem((X, Y, ROWS, NB), BF16), vmem((X, Y, ROWS, NB), BF16),
             vmem((Y, ROWS, NB), BF16), vmem((Y, ROWS, NB), BF16),
             vmem((X, Z, C, SUB, NB), F32), vmem((X, Z, SUB, NB), BF16), vmem((X, Z, SUB, NB), BF16),
             vmem((X, Z, SUB, NB), BF16), vmem((X, Z, SUB, NB), BF16),
             vmem((X, SUB, NB), F32), vmem((X, SUB, NB), F32),
-            dma((2, Y)), dma((2 + X,)), dma((X,)), dma((X,)), dma((X, Y)), dma((X, Y)),
+            dma((2, Y)), dma((3 + X,)), dma((X,)), dma((X,)), dma((X, Y)), dma((X, Y)),
             dma((Z,)), dma((Z,)), dma((Z,)), dma((Z,)), dma((X, Y)), dma((X, Y)),
-            dma((X,)), dma((X,)), dma((Y,)), dma((Y,)), dma((X,)), dma((X,)),
+            dma((X, 2)), dma((X, 2)), dma((Y,)), dma((Y,)), dma((X,)), dma((X,)),
             dma((X, Z)), dma((X, Z)), dma((X,)), dma((X,)),
         ],
         compiler_params=pltpu.CompilerParams(
@@ -272,7 +283,7 @@
         ),
         cost_estimate=pl.CostEstimate(flops=4 * ROWS * NPTS * NOCC, bytes_accessed=5 * 2**20, transcendentals=X * NOCC),
         name="response_backward",
-    )(chi_grad[0], green_unocc[0], orbitals, tau_points, energy.reshape(1, NOCC))
+    )(chi_grad[0], green_unocc[0], orbitals, tau_points, energy)
 
 
 def solution(mesh):

time: 77.6 us -> 69.8 us (0.90)
  Pallas kernels: 73.9 us -> 67.4 us
  local copies, waits for them, and re-layouts: 2.91 us -> 1.62 us
    pallas_call x1, Pallas kernels: 73.9 us -> 67.4 us  [per_device(): pl.pallas_call(kernel, out_shape=jax.ShapeDtypeStruct((ROWS, NB), F32), i...]
    reshape x1 -> x0, local copies, waits for them, and re-layouts: 1.29 us -> none  [per_device(): energy.reshape(1, NOCC)]
where the time goes in v3:
time: 69.8 us; the launch traced here: 69.7 us
  Pallas kernels  67.4 us (97%)
  local copies, waits for them, and re-layouts  1.62 us (2%)
    pallas_call x1, Pallas kernels, per_device(): pl.pallas_call(kernel, out_shape=jax.ShapeDtypeStruct((ROWS, NB), F32), i...  67.4 us
    unnamed x1, local copies, waits for them, and re-layouts  1.62 us

profile of v3, /device:TPU:1, one launch (start us, length us, event | category | flops | bytes accessed | tf_op | source)
XLA Modules:
  0.0 69.7 jit_solution(7570707336692125457)
XLA Ops:
  0.7 67.4 %response_backward.1 = f32[128,384]{1,0:T(8,128)} custom-call(bf16[128,8192]{1,0:T(8,128)(2,1)} %bitcast.2, bf16[128,8192]{1,0:T(8,128)(2,1)} %bitcast.3, bf16[128,1536]{1,0:T(8,128)(2,1)} %orb.1, f32[1]{0:T(128)S(6)} %copy.7.tau, f32[1536]{0:T(1024)} %energy.1), custom_call_target="tpu_custom_call" | custom-call | flops 6442450944 | bytes 5242880 | tf_op jit(solution)/shard_map/response_backward/pallas_call | solution.py:257
  68.1 1.6 %copy.8 = f32[128,384]{1,0:T(8,128)} copy(f32[128,384]{1,0:T(8,128)} %response_backward.1) | data formatting | bytes 393216

commit v4 on v3

--- a/solution.py
+++ b/solution.py
@@ -52,7 +52,7 @@
         for cp in loads[dy]:
             cp.start()
     mine = orb.at[pl.ds(pl.multiple_of(x * SUB, SUB), SUB)]
-    own = [pltpu.make_async_copy(mine, orb_c.at[q], own_sem.at[0])]
+    own = [pltpu.make_async_copy(mine, orb_c.at[z, c], own_sem.at[0])]
     for k in range(X):
         own.append(pltpu.make_async_copy(orb.at[:, nblock(k)], orb_r.at[k, 0], own_sem.at[2 + k]))
     own.append(pltpu.make_async_copy(energy, levels, own_sem.at[2 + X]))
@@ -85,58 +85,56 @@
             for k in range(X):
                 sbuf[dy, k, :, g * ROWS:(g + 1) * ROWS] = packed[g * ROWS:(g + 1) * ROWS, k * ROWS:(k + 1) * ROWS]
 
-    sent = []
-
     def go(cp):
         cp.start()
-        sent.append(cp)
         return cp
+
+    def drain(ref, sem):
+        pltpu.make_async_copy(ref, ref, sem).wait()
 
     aa_in = {}
 
     def send_block(dx, dy):
         part = sbuf.at[dy, (x + dx) % X]
         if dx or dy:
-            cp = remote(part, blocks.at[dx, dy], aa_s.at[dx, dy], aa_r.at[dx, dy], at(dx, dy))
+            cp = remote(part, blocks.at[dx, dy], aa_s.at[min(dx, 1)], aa_r.at[dx, dy], at(dx, dy))
         else:
             cp = pltpu.make_async_copy(part, blocks.at[0, 0], own_sem.at[1])
         cp.start()
         aa_in[dx, dy] = cp
 
-    or_in = {}
-
     def send_orb(k):
         for dy in (2, 1, 3):
-            or_in[k, dy] = go(
-                remote(orb.at[:, nblock(k)], orb_r.at[k, dy], or_s.at[k, dy], or_r.at[k, dy], at(dy=dy))
-            )
+            go(remote(orb.at[:, nblock(k)], orb_r.at[k, dy], or_s, or_r.at[k], at(dy=dy)))
 
     taus[0] = jnp.full((8, 128), tau[0], F32)
     make(2)
+    pl.semaphore_wait(barrier, X * Y - 1 + Z - 1 + 1)
+    send_block(0, 2)
+    send_block(2, 2)
+    oc_in = {dz: go(remote(mine, orb_c.at[z, c], oc_s, oc_r.at[dz], at(dz=dz))) for dz in (4, 3, 5, 2, 6, 1, 7)}
+    go(remote(mine, orb_c.at[z, c], os_s, os_r, at(flip=True)))
+    for dx in range(1, X):
+        go(remote(taus.at[0], taus.at[dx], tau_s, tau_r, at(dx=dx)))
     make(1)
+    send_block(0, 1)
+    send_block(1, 1)
     make(3)
-    pl.semaphore_wait(barrier, X * Y - 1 + Z - 1 + 1)
-    tau_in = [go(remote(taus.at[0], taus.at[dx], tau_s.at[dx], tau_r.at[dx], at(dx=dx))) for dx in range(1, X)]
-    for dx, dy in ((0, 2), (2, 2), (0, 1), (0, 3), (1, 1), (3, 3), (1, 3), (3, 1), (1, 2), (3, 2), (2, 1), (2, 3)):
+    for dx, dy in ((0, 3), (3, 3), (1, 3), (3, 1), (1, 2), (3, 2), (2, 1), (2, 3)):
         send_block(dx, dy)
     make(0)
     for dx in (2, 1, 3, 0):
         send_block(dx, 0)
     send_orb(1)
-    oc_in = {
-        dz: go(remote(mine, orb_c.at[q], oc_s.at[dz], oc_r.at[dz], at(dz=dz))) for dz in (4, 3, 5, 2, 6, 1, 7)
-    }
-    os_in = [go(remote(mine, orb_c.at[q], os_s.at[0], os_r.at[0], at(flip=True)))]
 
     for cp in own:
         cp.wait()
     for dz in (1, 7, 2, 6, 3, 5, 4):
         oc_in[dz].wait_recv()
-        slot = ((z - dz) % Z) * C + c
-        os_in.append(go(remote(orb_c.at[slot], orb_c.at[slot], os_s.at[dz], os_r.at[dz], at(flip=True))))
+        slot = orb_c.at[(z - dz) % Z, c]
+        go(remote(slot, slot, os_s, os_r, at(flip=True)))
     send_orb(2)
-    for cp in tau_in:
-        cp.wait_recv()
+    drain(taus.at[pl.ds(1, X - 1)], tau_r)
 
     def arrive(dx, dy):
         if dx or dy:
@@ -145,32 +143,29 @@
             aa_in[0, 0].wait()
         blocks_t[dx, :, dy * ROWS:(dy + 1) * ROWS] = blocks[dx, dy].T
 
-    sib_in, p2_in, px_in = {}, {}, {}
+    sib_in = {}
 
     def weight(dx, k):
         return jnp.exp(-taus[dx][:1, :1] * levels[nblock(k)].reshape(1, NB))
 
     def cols_part(k):
-        for dy in (1, 3, 2):
-            or_in[k, dy].wait_recv()
+        drain(orb_r.at[k, pl.ds(1, Y - 1)], or_r.at[k])
         rhs = orb_r[k].reshape(Y * ROWS, NB)
         acc = 0.0
         for dx in range(X):
             acc += jnp.dot(blocks_t[dx], rhs, preferred_element_type=F32) * weight(dx, k)
         p2[k] = acc.reshape(Z, C, SUB, NB)
         p2_sib[k] = p2[k, :, 1 - c].astype(BF16)
-        sib_in[k] = go(remote(p2_sib.at[k], p2_rx.at[k], sib_s.at[k], sib_r.at[k], at(flip=True)))
+        sib_in[k] = go(remote(p2_sib.at[k], p2_rx.at[k], sib_s, sib_r.at[k], at(flip=True)))
 
     def cols_send(k):
         sib_in[k].wait_recv()
         p2_tx[k] = (p2[k, :, c] + p2_rx[k].astype(F32)).astype(BF16)
         for dz in (4, 3, 5, 2, 6, 1, 7):
-            p2_in[k, dz] = go(
-                remote(p2_tx.at[k, (z + dz) % Z], r2.at[k, dz], p2_s.at[k, dz], p2_r.at[k, dz], at(dz=dz))
-            )
+            go(remote(p2_tx.at[k, (z + dz) % Z], r2.at[k, dz], p2_s, p2_r.at[k], at(dz=dz)))
 
     def rows_part(k):
-        rhs = orb_c[:, :, nblock(k)].reshape(COLS, NB)
+        rhs = orb_c[:, :, :, nblock(k)].reshape(COLS, NB)
         acc = 0.0
         for dx in range(X):
             acc += jnp.dot(blocks[dx].reshape(Y * ROWS, COLS), rhs, preferred_element_type=F32) * weight(dx, k)
@@ -180,21 +175,13 @@
 
     def rows_send(k, first, count):
         part = pl.ds(first, count)
-        px_in[k, first] = go(
-            remote(p1.at[k, part], r1x.at[k, part], px_s.at[k, first], px_r.at[k, first], at(dx=k))
-        )
+        go(remote(p1.at[k, part], r1x.at[k, part], px_s.at[first], px_r.at[first], at(dx=k)))
 
     for dx, dy in aa_in:
         arrive(dx, dy)
-    for dx, dy in aa_in:
-        if dx or dy:
-            aa_in[dx, dy].wait_send()
-    for cp in os_in:
-        cp.wait_recv()
+    drain(orb_c.at[:, 1 - c], os_r)
     for k in (3, 0):
         send_orb(k)
-
-    py_in = []
 
     def rows_sum(dy):
         total = p1[0, dy].astype(F32)
@@ -202,25 +189,25 @@
             total += r1x[k, dy].astype(F32)
         if dy:
             p1y[dy] = total.astype(BF16)
-            py_in.append(go(remote(p1y.at[dy], r1y.at[dy], py_s.at[dy], py_r.at[dy], at(dy=-dy))))
+            go(remote(p1y.at[dy], r1y.at[dy], py_s, py_r, at(dy=-dy)))
         else:
             out[...] = total
 
     def cols_sum(k):
         total = p2_tx[k, z].astype(F32)
-        for dz in (1, 7, 2, 6, 3, 5, 4):
-            p2_in[k, dz].wait_recv()
+        drain(r2.at[k, pl.ds(1, Z - 1)], p2_r.at[k])
+        for dz in range(1, Z):
             total += r2[k, dz].astype(F32)
         f_tx[k] = total
         if k:
-            return go(remote(f_tx.at[k], f_rx.at[k], f_s.at[k], f_r.at[k], at(dx=k)))
-
+            go(remote(f_tx.at[k], f_rx.at[k], f_s, f_r, at(dx=k)))
+
+    rows_part(2)
+    rows_part(1)
     cols_part(1)
-    rows_part(2)
+    rows_part(3)
     cols_send(1)
-    rows_part(1)
     cols_part(2)
-    rows_part(3)
     cols_send(2)
     cols_part(3)
     rows_part(0)
@@ -228,27 +215,36 @@
     for k in (2, 1, 3):
         rows_send(k, 0, 1)
     cols_part(0)
-    f_in = [cols_sum(1)]
+    cols_sum(1)
     cols_send(0)
-    for k in range(1, X):
-        px_in[k, 1].wait_recv()
+    others = pl.ds(1, X - 1)
+    rest = pl.ds(1, Y - 1)
+    drain(r1x.at[others, rest], px_r.at[1])
     for dy in (2, 1, 3):
         rows_sum(dy)
-    f_in.append(cols_sum(2))
-    f_in.append(cols_sum(3))
+    cols_sum(2)
+    cols_sum(3)
+    drain(r1x.at[others, pl.ds(0, 1)], px_r.at[0])
+    rows_sum(0)
+    drain(r1y.at[rest], py_r)
+    out[...] += r1y[1].astype(F32) + r1y[2].astype(F32) + r1y[3].astype(F32)
+    drain(f_rx.at[others], f_r)
     for k in range(1, X):
-        px_in[k, 0].wait_recv()
-    rows_sum(0)
-    for cp in py_in:
-        cp.wait_recv()
-    out[...] += r1y[1].astype(F32) + r1y[2].astype(F32) + r1y[3].astype(F32)
-    for k in range(1, X):
-        f_in[k - 1].wait_recv()
         out[pl.ds(pl.multiple_of(((x - k) % X) * SUB, SUB), SUB)] += f_rx[k]
     cols_sum(0)
     out[pl.ds(pl.multiple_of(x * SUB, SUB), SUB)] += f_tx[0]
-    for cp in sent:
-        cp.wait_send()
+    drain(taus.at[others], tau_s)
+    drain(orb_c.at[pl.ds(1, Z - 1), 0], oc_s)
+    drain(orb_c.at[:, 0], os_s)
+    drain(blocks.at[0, rest], aa_s.at[0])
+    drain(blocks.at[others], aa_s.at[1])
+    drain(orb_r.at[:, rest], or_s)
+    drain(p2_rx, sib_s)
+    drain(r2.at[:, pl.ds(1, Z - 1)], p2_s)
+    drain(r1x.at[others, pl.ds(0, 1)], px_s.at[0])
+    drain(r1x.at[others, rest], px_s.at[1])
+    drain(r1y.at[rest], py_s)
+    drain(f_rx.at[others], f_s)
 
 
 def per_device(chi_grad, green_unocc, orbitals, tau_points, energy):
@@ -266,17 +262,15 @@
         scratch_shapes=[
             vmem((Y, ROWS, SPAN), BF16), vmem((Y, ROWS, SPAN), BF16), vmem((SPAN // GROUP, ROWS, GROUP), BF16),
             vmem((Y, X, ROWS, COLS), BF16), vmem((X, Y, ROWS, COLS), BF16), vmem((X, COLS, Y * ROWS), BF16),
-            vmem((X, Y, ROWS, NB), BF16), vmem((Z * C, SUB, NOCC), BF16), vmem((X, 8, 128), F32),
+            vmem((X, Y, ROWS, NB), BF16), vmem((Z, C, SUB, NOCC), BF16), vmem((X, 8, 128), F32),
             vmem((NOCC,), F32),
             vmem((X, Y, ROWS, NB), BF16), vmem((X, Y, ROWS, NB), BF16),
             vmem((Y, ROWS, NB), BF16), vmem((Y, ROWS, NB), BF16),
             vmem((X, Z, C, SUB, NB), F32), vmem((X, Z, SUB, NB), BF16), vmem((X, Z, SUB, NB), BF16),
             vmem((X, Z, SUB, NB), BF16), vmem((X, Z, SUB, NB), BF16),
             vmem((X, SUB, NB), F32), vmem((X, SUB, NB), F32),
-            dma((2, Y)), dma((3 + X,)), dma((X,)), dma((X,)), dma((X, Y)), dma((X, Y)),
-            dma((Z,)), dma((Z,)), dma((Z,)), dma((Z,)), dma((X, Y)), dma((X, Y)),
-            dma((X, 2)), dma((X, 2)), dma((Y,)), dma((Y,)), dma((X,)), dma((X,)),
-            dma((X, Z)), dma((X, Z)), dma((X,)), dma((X,)),
+            dma((2, Y)), dma((3 + X,)), dma, dma, dma, dma((X,)), dma, dma((Z,)), dma, dma, dma((2,)), dma((X, Y)),
+            dma((2,)), dma((2,)), dma, dma, dma, dma((X,)), dma, dma((X,)), dma, dma,
         ],
         compiler_params=pltpu.CompilerParams(
             collective_id=1, has_side_effects=True, vmem_limit_bytes=56 * 2**20

time: 69.8 us -> 65.8 us (0.943)
  Pallas kernels: 67.4 us -> 63.4 us
    pallas_call x1, Pallas kernels: 67.4 us -> 63.4 us  [per_device(): pl.pallas_call(kernel, out_shape=jax.ShapeDtypeStruct((ROWS, NB), F32), i...]
where the time goes in v4:
time: 65.8 us; the launch traced here: 65.7 us
  Pallas kernels  63.4 us (96%)
  local copies, waits for them, and re-layouts  1.62 us (2%)
  between operations  0.66 us (1%)
    pallas_call x1, Pallas kernels, per_device(): pl.pallas_call(kernel, out_shape=jax.ShapeDtypeStruct((ROWS, NB), F32), i...  63.4 us
    unnamed x1, local copies, waits for them, and re-layouts  1.62 us

profile of v4, /device:TPU:1, one launch (start us, length us, event | category | flops | bytes accessed | tf_op | source)
XLA Modules:
  0.0 65.7 jit_solution(11904078684904866389)
XLA Ops:
  0.7 63.4 %response_backward.1 = f32[128,384]{1,0:T(8,128)} custom-call(bf16[128,8192]{1,0:T(8,128)(2,1)} %bitcast.2, bf16[128,8192]{1,0:T(8,128)(2,1)} %bitcast.3, bf16[128,1536]{1,0:T(8,128)(2,1)} %orb.1, f32[1]{0:T(128)S(6)} %copy.7.tau, f32[1536]{0:T(1024)} %energy.1), custom_call_target="tpu_custom_call" | custom-call | flops 6442450944 | bytes 5242880 | tf_op jit(solution)/shard_map/response_backward/pallas_call | solution.py:253
  64.1 1.6 %copy.8 = f32[128,384]{1,0:T(8,128)} copy(f32[128,384]{1,0:T(8,128)} %response_backward.1) | data formatting | bytes 393216

commit v5 on v4

--- a/solution.py
+++ b/solution.py
@@ -215,13 +215,13 @@
     for k in (2, 1, 3):
         rows_send(k, 0, 1)
     cols_part(0)
-    cols_sum(1)
-    cols_send(0)
     others = pl.ds(1, X - 1)
     rest = pl.ds(1, Y - 1)
     drain(r1x.at[others, rest], px_r.at[1])
     for dy in (2, 1, 3):
         rows_sum(dy)
+    cols_send(0)
+    cols_sum(1)
     cols_sum(2)
     cols_sum(3)
     drain(r1x.at[others, pl.ds(0, 1)], px_r.at[0])
@@ -252,7 +252,7 @@
     hbm = pl.BlockSpec(memory_space=pl.ANY)
     return pl.pallas_call(
         kernel,
-        out_shape=jax.ShapeDtypeStruct((ROWS, NB), F32),
+        out_shape=pltpu.VMEM((ROWS, NB), F32),
         in_specs=[
             hbm, hbm, hbm,
             pl.BlockSpec(memory_space=pltpu.SMEM),

time: 65.8 us -> 64.2 us (0.976)
  local copies, waits for them, and re-layouts: 1.62 us -> 0.68 us
  Pallas kernels: 63.4 us -> 62.7 us
    unnamed x1, local copies, waits for them, and re-layouts: 1.62 us -> 0.68 us
    pallas_call x1, Pallas kernels: 63.4 us -> 62.7 us  [per_device(): pl.pallas_call(kernel, out_shape=pltpu.VMEM((ROWS, NB), F32), in_specs=[h...]
where the time goes in v5:
time: 64.2 us; the launch traced here: 64.1 us
  Pallas kernels  62.7 us (98%)
  local copies, waits for them, and re-layouts  0.68 us (1%)
  between operations  0.66 us (1%)
    pallas_call x1, Pallas kernels, per_device(): pl.pallas_call(kernel, out_shape=pltpu.VMEM((ROWS, NB), F32), in_specs=[h...  62.7 us

profile of v5, /device:TPU:1, one launch (start us, length us, event | category | flops | bytes accessed | tf_op | source)
XLA Modules:
  0.0 64.1 jit_solution(13287332768112724666)
XLA Ops:
  0.7 62.7 %response_backward.1 = f32[128,384]{1,0:T(8,128)S(1)} custom-call(bf16[128,8192]{1,0:T(8,128)(2,1)} %bitcast.2, bf16[128,8192]{1,0:T(8,128)(2,1)} %bitcast.3, bf16[128,1536]{1,0:T(8,128)(2,1)} %orb.1, f32[1]{0:T(128)S(6)} %copy.8.tau, f32[1536]{0:T(1024)} %energy.1), custom_call_target="tpu_custom_call" | custom-call | flops 6442450944 | bytes 5242880 | tf_op jit(solution)/shard_map/response_backward/pallas_call | solution.py:253
  63.4 0.7 %copy.7 = f32[128,384]{1,0:T(8,128)} copy(f32[128,384]{1,0:T(8,128)S(1)} %response_backward.1) | data formatting | bytes 393216

commit v6 on v5

--- a/solution.py
+++ b/solution.py
@@ -122,10 +122,10 @@
     make(3)
     for dx, dy in ((0, 3), (3, 3), (1, 3), (3, 1), (1, 2), (3, 2), (2, 1), (2, 3)):
         send_block(dx, dy)
+    send_orb(1)
     make(0)
     for dx in (2, 1, 3, 0):
         send_block(dx, 0)
-    send_orb(1)
 
     for cp in own:
         cp.wait()
@@ -203,11 +203,11 @@
             go(remote(f_tx.at[k], f_rx.at[k], f_s, f_r, at(dx=k)))
 
     rows_part(2)
+    cols_part(1)
     rows_part(1)
-    cols_part(1)
-    rows_part(3)
     cols_send(1)
     cols_part(2)
+    rows_part(3)
     cols_send(2)
     cols_part(3)
     rows_part(0)

time: 64.2 us -> 63.6 us (level)
  Pallas kernels: 62.7 us -> 61.8 us
    pallas_call x1, Pallas kernels: 62.7 us -> 61.8 us  [per_device(): pl.pallas_call(kernel, out_shape=pltpu.VMEM((ROWS, NB), F32), in_specs=[h...]
where the time goes in v6:
time: 63.6 us; the launch traced here: 63.2 us
  Pallas kernels  61.8 us (97%)
  local copies, waits for them, and re-layouts  0.68 us (1%)
  between operations  0.66 us (1%)
    pallas_call x1, Pallas kernels, per_device(): pl.pallas_call(kernel, out_shape=pltpu.VMEM((ROWS, NB), F32), in_specs=[h...  61.8 us

profile of v6, /device:TPU:1, one launch (start us, length us, event | category | flops | bytes accessed | tf_op | source)
XLA Modules:
  0.0 63.2 jit_solution(9960716394662687281)
XLA Ops:
  0.7 61.8 %response_backward.1 = f32[128,384]{1,0:T(8,128)S(1)} custom-call(bf16[128,8192]{1,0:T(8,128)(2,1)} %bitcast.2, bf16[128,8192]{1,0:T(8,128)(2,1)} %bitcast.3, bf16[128,1536]{1,0:T(8,128)(2,1)} %orb.1, f32[1]{0:T(128)S(6)} %copy.8.tau, f32[1536]{0:T(1024)} %energy.1), custom_call_target="tpu_custom_call" | custom-call | flops 6442450944 | bytes 5242880 | tf_op jit(solution)/shard_map/response_backward/pallas_call | solution.py:253
  62.5 0.7 %copy.7 = f32[128,384]{1,0:T(8,128)} copy(f32[128,384]{1,0:T(8,128)S(1)} %response_backward.1) | data formatting | bytes 393216

commit v7 on v6

--- a/solution.py
+++ b/solution.py
@@ -20,7 +20,7 @@
 
 def kernel(
     chi, green, orb, tau, energy, out,
-    chi_v, green_v, occ_v, sbuf, blocks, blocks_t, orb_r, orb_c, taus, levels,
+    chi_v, green_v, occ_v, sbuf, blocks, blocks_t, orb_r, orb_c, taus, levels, tau_v,
     p1, r1x, p1y, r1y, p2, p2_sib, p2_rx, p2_tx, r2, f_tx, f_rx,
     load_sem, own_sem, tau_s, tau_r, or_s, or_r, oc_s, oc_r, os_s, os_r, aa_s, aa_r,
     px_s, px_r, py_s, py_r, sib_s, sib_r, p2_s, p2_r, f_s, f_r,
@@ -56,6 +56,8 @@
     for k in range(X):
         own.append(pltpu.make_async_copy(orb.at[:, nblock(k)], orb_r.at[k, 0], own_sem.at[2 + k]))
     own.append(pltpu.make_async_copy(energy, levels, own_sem.at[2 + X]))
+    tau_in = pltpu.make_async_copy(tau, tau_v, own_sem.at[3 + X])
+    tau_in.start()
     for cp in own:
         cp.start()
 
@@ -107,8 +109,9 @@
         for dy in (2, 1, 3):
             go(remote(orb.at[:, nblock(k)], orb_r.at[k, dy], or_s, or_r.at[k], at(dy=dy)))
 
-    taus[0] = jnp.full((8, 128), tau[0], F32)
     make(2)
+    tau_in.wait()
+    taus[0] = jnp.full((8, 128), tau_v[0], F32)
     pl.semaphore_wait(barrier, X * Y - 1 + Z - 1 + 1)
     send_block(0, 2)
     send_block(2, 2)
@@ -255,21 +258,20 @@
         out_shape=pltpu.VMEM((ROWS, NB), F32),
         in_specs=[
             hbm, hbm, hbm,
-            pl.BlockSpec(memory_space=pltpu.SMEM),
-            hbm,
+            hbm, hbm,
         ],
         out_specs=pl.BlockSpec(memory_space=pltpu.VMEM),
         scratch_shapes=[
             vmem((Y, ROWS, SPAN), BF16), vmem((Y, ROWS, SPAN), BF16), vmem((SPAN // GROUP, ROWS, GROUP), BF16),
             vmem((Y, X, ROWS, COLS), BF16), vmem((X, Y, ROWS, COLS), BF16), vmem((X, COLS, Y * ROWS), BF16),
             vmem((X, Y, ROWS, NB), BF16), vmem((Z, C, SUB, NOCC), BF16), vmem((X, 8, 128), F32),
-            vmem((NOCC,), F32),
+            vmem((NOCC,), F32), pltpu.SMEM((1,), F32),
             vmem((X, Y, ROWS, NB), BF16), vmem((X, Y, ROWS, NB), BF16),
             vmem((Y, ROWS, NB), BF16), vmem((Y, ROWS, NB), BF16),
             vmem((X, Z, C, SUB, NB), F32), vmem((X, Z, SUB, NB), BF16), vmem((X, Z, SUB, NB), BF16),
             vmem((X, Z, SUB, NB), BF16), vmem((X, Z, SUB, NB), BF16),
             vmem((X, SUB, NB), F32), vmem((X, SUB, NB), F32),
-            dma((2, Y)), dma((3 + X,)), dma, dma, dma, dma((X,)), dma, dma((Z,)), dma, dma, dma((2,)), dma((X, Y)),
+            dma((2, Y)), dma((4 + X,)), dma, dma, dma, dma((X,)), dma, dma((Z,)), dma, dma, dma((2,)), dma((X, Y)),
             dma((2,)), dma((2,)), dma, dma, dma, dma((X,)), dma, dma((X,)), dma, dma,
         ],
         compiler_params=pltpu.CompilerParams(

time: 63.6 us -> 63.6 us (level)
  no operation moved by 1% of the time
where the time goes in v7:
time: 63.6 us; the launch traced here: 63.2 us
  Pallas kernels  61.9 us (97%)
  local copies, waits for them, and re-layouts  0.68 us (1%)
  between operations  0.66 us (1%)
    pallas_call x1, Pallas kernels, per_device(): pl.pallas_call(kernel, out_shape=pltpu.VMEM((ROWS, NB), F32), in_specs=[h...  61.9 us

profile of v7, /device:TPU:1, one launch (start us, length us, event | category | flops | bytes accessed | tf_op | source)
XLA Modules:
  0.0 63.2 jit_solution(10423153461941231355)
XLA Ops:
  0.7 61.9 %response_backward.1 = f32[128,384]{1,0:T(8,128)S(1)} custom-call(bf16[128,8192]{1,0:T(8,128)(2,1)} %bitcast.2, bf16[128,8192]{1,0:T(8,128)(2,1)} %bitcast.3, bf16[128,1536]{1,0:T(8,128)(2,1)} %orb.1, f32[1]{0:T(128)S(6)} %copy.8.tau, f32[1536]{0:T(1024)} %energy.1), custom_call_target="tpu_custom_call" | custom-call | flops 6442450944 | bytes 5242880 | tf_op jit(solution)/shard_map/response_backward/pallas_call | solution.py:256
  62.5 0.7 %copy.7 = f32[128,384]{1,0:T(8,128)} copy(f32[128,384]{1,0:T(8,128)S(1)} %response_backward.1) | data formatting | bytes 393216
